TPU v7x, 32 devices: a whole 2x2x4 slice. The times are simulated.
32 devices in a mesh: groups: 2 (over x), dp: 16 (over z, y, core).
Axes of the slice: x: 2, y: 2, z: 4, core: 2. Of those that a mesh axis runs over, the one named last changes fastest.
Arguments:
- patches: bfloat16 [16384, 1280], P(('groups', 'dp')), parts along dimension 0, may hold values from -8 to 8
- send_index: int32 [32, 16, 32], P(('groups', 'dp')), parts along dimension 0, may hold values from -1 to 511, as said below
- window_id: int32 [16384], P(('groups', 'dp')), parts along dimension 0, may hold values from -1 to 8, as said below
- norm_gain: float32 [1280], replicated, may hold values from 0.5 to 5
- w_qkv: bfloat16 [1280, 1920], replicated, may hold values from -0.15625 to 0.15625
- w_proj: bfloat16 [640, 1280], replicated, may hold values from -0.25 to 0.25
- out_grad: bfloat16 [16384, 1280], P(('groups', 'dp')), parts along dimension 0, may hold values from -6 to 6
Outputs:
- embeds: bfloat16 [16384, 1280], P(('groups', 'dp')), parts along dimension 0
- patch_grad: bfloat16 [16384, 1280], P(('groups', 'dp')), parts along dimension 0
- qkv_grad: float32 [2560, 1920], P(('groups', 'dp')), parts along dimension 0
- proj_grad: float32 [1280, 1280], P('groups', 'dp'), parts along dimension 0
There are 2 independent parts, one for each index of `groups`. A program takes and returns all parts, laid end to end along the dimension named above; an argument that names none is the same for every part. Nothing has to cross between parts.
Inputs may be any that keep to these rules, and one draw needn't show every extreme that they name: send_index[s, d, c] is the row of device s that fills slot c of device d, -1 for an empty slot. The filled slots of each pair come first; the rows below the number of filled slots of device s are each sent exactly once and the rows above are sent nowhere. Some device receives 32 rows from every device and some device sends 32 rows to every device. window_id is -1 exactly on empty received slots; the windows of a device are numbered from 0 without gaps and hold at most 64 slots each, spread over the device's slots.
All inputs are finite; a program needn't handle non-finite values.
Results may differ from a plain program's by a relative error of at most 0.0055.
The roundings to bfloat16 on the way count: a program that leaves them out, or rounds other values in their place, can miss the bound.
Values may be sent and summed in bfloat16 or wider, within the bound.
A program may use at most 128 MiB of HBM per device.

v0:
```python
import math

import jax
import jax.numpy as jnp
from jax import lax
from jax.sharding import PartitionSpec as P

HEADS = 8
HDIM = 80


def contract_rows(left, right):
    return lax.dot_general(
        left, right, (((0,), (0,)), ((), ())), preferred_element_type=jnp.float32
    )


def contract_cols(left, right):
    return lax.dot_general(
        left, right, (((1,), (1,)), ((), ())), preferred_element_type=jnp.float32
    )


def shards(patches, send_index, window_id, norm_gain, w_qkv, w_proj, out_grad):
    peer_count = lax.axis_size("dp")
    slot_count = patches.shape[0]
    per_peer = send_index.shape[2]
    width = patches.shape[1]
    heads = HEADS
    head_size = HDIM
    inner_width = heads * head_size
    qkv_width = 3 * inner_width
    score_scale = 1.0 / math.sqrt(head_size)
    grad_scale = 1.0 / math.sqrt(slot_count * peer_count)
    send_rows = send_index[0]
    slot_live = send_rows >= 0
    safe_rows = jnp.maximum(send_rows, 0).reshape(-1)

    def pack(rows):
        picked = jnp.take(rows, safe_rows, axis=0).reshape(peer_count, per_peer, width)
        return jnp.where(slot_live[:, :, None], picked, jnp.zeros((), rows.dtype))

    def unpack(rows):
        target = jnp.where(slot_live, send_rows, slot_count).reshape(-1)
        flat_rows = rows.reshape(peer_count * per_peer, width)
        return jnp.zeros((slot_count, width), jnp.bfloat16).at[target].set(flat_rows, mode="drop")

    sent_rows, sent_grads = (
        lax.all_to_all(pack(patches), "dp", split_axis=0, concat_axis=0, tiled=True),
        lax.all_to_all(pack(out_grad), "dp", split_axis=0, concat_axis=0, tiled=True),
    )
    gathered = sent_rows.reshape(slot_count, width)
    grad_in = sent_grads.reshape(slot_count, width)
    row_vals = gathered.astype(jnp.float32)
    inv_rms = lax.rsqrt(jnp.mean(row_vals * row_vals, axis=-1, keepdims=True) + 1e-06)
    unit = row_vals * inv_rms
    normed = (unit * norm_gain).astype(jnp.bfloat16)
    qkv = jnp.dot(normed, w_qkv, preferred_element_type=jnp.float32).astype(jnp.bfloat16)
    qkv = qkv.reshape(slot_count, 3, heads, head_size)
    queries, keys, values = (qkv[:, 0], qkv[:, 1], qkv[:, 2])
    same_window = window_id[:, None] == window_id[None, :]
    scores = (
        jnp.einsum("qhd,khd->hqk", queries, keys, preferred_element_type=jnp.float32) * score_scale
    )
    scores = jnp.where(same_window[None], scores, -1e30)
    top = jnp.max(scores, axis=-1, keepdims=True)
    expo = jnp.exp(scores - top)
    probs = expo / jnp.sum(expo, axis=-1, keepdims=True)
    probs_low = probs.astype(jnp.bfloat16)
    attended = jnp.einsum("hqk,khd->qhd", probs_low, values, preferred_element_type=jnp.float32)
    attended = attended.astype(jnp.bfloat16).reshape(slot_count, inner_width)
    mixed = (row_vals + jnp.dot(attended, w_proj, preferred_element_type=jnp.float32)).astype(
        jnp.bfloat16
    )
    proj_term = contract_rows(attended, grad_in) * grad_scale
    d_att = (
        contract_cols(grad_in, w_proj).astype(jnp.bfloat16).reshape(slot_count, heads, head_size)
    )
    d_probs = jnp.einsum("qhd,khd->hqk", d_att, values, preferred_element_type=jnp.float32)
    d_scores = probs * (d_probs - jnp.sum(probs * d_probs, axis=-1, keepdims=True)) * score_scale
    d_scores = d_scores.astype(jnp.bfloat16)
    d_query = jnp.einsum("hqk,khd->qhd", d_scores, keys, preferred_element_type=jnp.float32)
    d_key = jnp.einsum("hqk,qhd->khd", d_scores, queries, preferred_element_type=jnp.float32)
    d_value = jnp.einsum("hqk,qhd->khd", probs_low, d_att, preferred_element_type=jnp.float32)
    d_qkv = (
        jnp.stack([d_query, d_key, d_value], axis=1)
        .astype(jnp.bfloat16)
        .reshape(slot_count, qkv_width)
    )
    qkv_term = contract_rows(normed, d_qkv) * grad_scale
    qkv_grad, proj_grad = (
        lax.psum_scatter(qkv_term, "dp", scatter_dimension=0, tiled=True),
        lax.psum_scatter(proj_term, "dp", scatter_dimension=1, tiled=True),
    )
    d_normed = contract_cols(d_qkv, w_qkv)
    scaled = d_normed * norm_gain
    d_rows = grad_in.astype(jnp.float32) + inv_rms * (
        scaled - unit * jnp.mean(scaled * unit, axis=-1, keepdims=True)
    )
    d_rows = d_rows.astype(jnp.bfloat16)
    back_out, back_grad = (
        lax.all_to_all(
            mixed.reshape(peer_count, per_peer, width),
            "dp",
            split_axis=0,
            concat_axis=0,
            tiled=True,
        ),
        lax.all_to_all(
            d_rows.reshape(peer_count, per_peer, width),
            "dp",
            split_axis=0,
            concat_axis=0,
            tiled=True,
        ),
    )
    embeds = unpack(back_out)
    patch_grad = unpack(back_grad)
    return (embeds, patch_grad, qkv_grad, proj_grad)


def solution(mesh):
    in_specs = (
        P(("groups", "dp"), None),
        P(("groups", "dp"), None, None),
        P(("groups", "dp")),
        P(),
        P(),
        P(),
        P(("groups", "dp"), None),
    )
    out_specs = (
        P(("groups", "dp"), None),
        P(("groups", "dp"), None),
        P(("groups", "dp"), None),
        P("groups", "dp"),
    )
    return jax.shard_map(shards, mesh=mesh, in_specs=in_specs, out_specs=out_specs, check_vma=False)
```

profile of v0, /device:TPU:0, one launch (start us, length us, event | category | flops | bytes accessed | tf_op | source)
XLA Modules:
  0.0 320.3 jit_solution(962615959419222842)
XLA Ops:
  8.8 5.5 %gather_fusion.1 = bf16[512,1280]{1,0:T(8,128)(2,1)} fusion(bf16[512,1280]{1,0:T(8,128)(2,1)} %param.15, s32[1024]{0:T(1024)S(1)} %pad_clamp_fusion), kind=kCustom, calls=%fused_computation.1.clone | custom fusion | bytes 2623488 | tf_op jit(solution)/shard_map/jit(_take)/gather | solution.py:40
  21.0 7.5 %all-to-all-start = ((bf16[16,32,1280]{2,1,0:T(8,128)(2,1)}), bf16[16,32,1280]{2,1,0:T(8,128)(2,1)S(1)}, u32[]{:S(2)}, u32[]{:S(2)}) async-start(bf16[16,32,1280]{2,1,0:T(8,128)(2,1)} %get-tuple-element.6), calls=%async_computation | async-start | bytes 2621440 | tf_op jit(solution)/shard_map/all_to_all | solution.py:49
  28.8 27.2 %all-to-all-done = bf16[16,32,1280]{2,1,0:T(8,128)(2,1)S(1)} async-done(((bf16[16,32,1280]{2,1,0:T(8,128)(2,1)}), bf16[16,32,1280]{2,1,0:T(8,128)(2,1)S(1)}, u32[]{:S(2)}, u32[]{:S(2)}) %all-to-all-start) | async-done | bytes 1310752 | tf_op jit(solution)/shard_map/all_to_all | solution.py:49
  56.0 8.2 %all-to-all-start.2 = ((bf16[16,32,1280]{2,1,0:T(8,128)(2,1)}), bf16[16,32,1280]{2,1,0:T(8,128)(2,1)}, u32[]{:S(2)}, u32[]{:S(2)}) async-start(bf16[16,32,1280]{2,1,0:T(8,128)(2,1)} %get-tuple-element.5), calls=%async_computation.2 | async-start | bytes 2621440 | tf_op jit(solution)/shard_map/all_to_all | solution.py:50
  65.0 6.5 %convolution_convert_fusion = bf16[512,1920]{1,0:T(8,128)(2,1)} fusion(bf16[512,1280]{1,0:T(8,128)(2,1)S(1)} %multiply_convert_fusion.2, bf16[1280,1920]{1,0:T(8,128)(2,1)} %param.13), kind=kOutput, calls=%fused_computation.24 | convolution fusion | flops 2517565440 | bytes 8192000 | tf_op jit(solution)/shard_map/dot_general | solution.py:58
  71.5 4.0 %copy.20 = bf16[512,1920]{0,1:T(8,128)(2,1)} copy(bf16[512,1920]{1,0:T(8,128)(2,1)} %convolution_convert_fusion) | data formatting | bytes 3932160 | tf_op jit(solution)/shard_map/convert_element_type | solution.py:58
  75.5 7.7 %fusion.46 = (f32[8,512]{1,0:T(8,128)S(1)}, f32[8,512,512]{1,2,0:T(8,128)}) fusion(pred[512,512]{0,1:T(8,128)(4,1)S(1)} %broadcast_compare_fusion, bf16[512,3,8,80]{0,3,2,1:T(8,128)(2,1)} %bitcast.85), kind=kOutput, calls=%fused_computation.70 | convolution fusion | flops 343933440 | bytes 9977856 | tf_op jit(solution)/shard_map/sub | solution.py:67
  83.2 5.3 %fusion.29 = bf16[8,80,512]{2,1,0:T(8,128)(2,1)} fusion(bf16[512,3,8,80]{0,3,2,1:T(8,128)(2,1)} %bitcast.86, f32[8,512,512]{1,2,0:T(8,128)} %get-tuple-element.10, f32[8,512]{1,0:T(8,128)S(1)} %get-tuple-element.9), kind=kOutput, calls=%fused_computation.38 | convolution fusion | flops 340066304 | bytes 9715712 | tf_op jit(solution)/shard_map/hqk,khd->qhd/dot_general | solution.py:70
  91.6 4.4 %convolution_multiply_fusion.1 = f32[640,1280]{0,1:T(8,128)} fusion(bf16[512,640]{0,1:T(8,128)(2,1)} %bitcast.94, bf16[512,1280]{1,0:T(8,128)(2,1)} %bitcast.13), kind=kOutput, calls=%fused_computation.20 | convolution fusion | flops 839680000 | bytes 5242880 | tf_op jit(solution)/shard_map/dot_general | solution.py:13
  96.3 3.4 %convolution_convert_fusion.1 = bf16[512,640]{1,0:T(8,128)(2,1)} fusion(bf16[512,1280]{1,0:T(8,128)(2,1)} %bitcast.13, bf16[640,1280]{1,0:T(8,128)(2,1)S(1)} %copy-done), kind=kOutput, calls=%fused_computation.39 | convolution fusion | flops 839188480 | bytes 3604480 | tf_op jit(solution)/shard_map/dot_general | solution.py:19
  101.9 5.8 %fusion.38 = f32[8,512,512]{1,2,0:T(8,128)} fusion(bf16[512,8,80]{0,2,1:T(8,128)(2,1)} %bitcast.90, bf16[512,3,8,80]{0,3,2,1:T(8,128)(2,1)} %bitcast.87), kind=kOutput, calls=%fused_computation.52 | convolution fusion | flops 335544320 | bytes 9699328 | tf_op jit(solution)/shard_map/qhd,khd->hqk/dot_general | solution.py:79
  107.7 15.9 %fusion.23 = bf16[512,1,8,80]{0,3,2,1:T(8,128)(2,1)} fusion(f32[8,512,512]{1,2,0:T(8,128)} %fusion.38, bf16[512,3,8,80]{0,3,2,1:T(8,128)(2,1)} %bitcast.88, f32[8,512,512]{1,2,0:T(8,128)} %get-tuple-element.10, f32[8,512]{1,0:T(8,128)S(1)} %get-tuple-element.9), kind=kOutput, calls=%fused_computation.36 | convolution fusion | flops 350228992 | bytes 34897920 | tf_op jit(solution)/shard_map/hqk,qhd->khd/dot_general | solution.py:83
  123.5 15.5 %fusion.20 = bf16[512,1,8,80]{0,3,2,1:T(8,128)(2,1)} fusion(f32[8,512,512]{1,2,0:T(8,128)} %fusion.38, bf16[512,3,8,80]{0,3,2,1:T(8,128)(2,1)} %bitcast.89, f32[8,512,512]{1,2,0:T(8,128)} %get-tuple-element.10, f32[8,512]{1,0:T(8,128)S(1)} %get-tuple-element.9), kind=kOutput, calls=%fused_computation.35 | convolution fusion | flops 350228992 | bytes 34897920 | tf_op jit(solution)/shard_map/hqk,khd->qhd/dot_general | solution.py:82
  139.1 5.2 %fusion.26 = bf16[512,1,8,80]{0,3,2,1:T(8,128)(2,1)S(1)} fusion(bf16[512,8,80]{0,2,1:T(8,128)(2,1)} %bitcast.91, f32[8,512,512]{1,2,0:T(8,128)} %get-tuple-element.10, f32[8,512]{1,0:T(8,128)S(1)} %get-tuple-element.9), kind=kOutput, calls=%fused_computation.37 | convolution fusion | flops 339738624 | bytes 9715712 | tf_op jit(solution)/shard_map/hqk,qhd->khd/dot_general | solution.py:84
  145.8 5.4 %convolution_multiply_fusion = f32[1280,1920]{1,0:T(8,128)} fusion(bf16[512,1280]{1,0:T(8,128)(2,1)S(1)} %bitcast.96, bf16[512,1920]{0,1:T(8,128)(2,1)S(1)} %bitcast.92), kind=kOutput, calls=%fused_computation.6 | convolution fusion | flops 2519040000 | bytes 13107200 | tf_op jit(solution)/shard_map/dot_general | solution.py:13
  151.2 3.4 %fusion.15 = bf16[512,1280]{1,0:T(8,128)(2,1)} fusion(bf16[512,640]{0,1:T(8,128)(2,1)} %bitcast.95, bf16[640,1280]{1,0:T(8,128)(2,1)S(1)} %copy-done, bf16[512,1280]{1,0:T(8,128)(2,1)S(1)} %bitcast.81), kind=kOutput, calls=%fused_computation.23 | convolution fusion | flops 840826880 | bytes 4915200 | tf_op jit(solution)/shard_map/dot_general | solution.py:72
  154.6 7.9 %all-to-all-start.1 = ((bf16[16,32,1280]{2,1,0:T(8,128)(2,1)}), bf16[16,32,1280]{2,1,0:T(8,128)(2,1)}, u32[]{:S(2)}, u32[]{:S(2)}) async-start(bf16[16,32,1280]{2,1,0:T(8,128)(2,1)} %bitcast.97), calls=%async_computation.1 | async-start | bytes 2621440 | tf_op jit(solution)/shard_map/all_to_all | solution.py:102
  162.5 6.2 %multiply_reduce_fusion.1 = (f32[512]{0:T(512)S(1)}, f32[512,1280]{1,0:T(8,128)S(1)}) fusion(bf16[16,32,1280]{2,1,0:T(8,128)(2,1)S(1)} %all-to-all-done, f32[512]{0:T(512)S(1)} %rsqrt.13, f32[1280]{0:T(1024)S(1)} %copy-done.6, bf16[512,1920]{0,1:T(8,128)(2,1)} %bitcast.93, bf16[1280,1920]{1,0:T(8,128)(2,1)} %param.13), kind=kOutput, calls=%fused_computation.28 | convolution fusion | flops 2519858688 | bytes 10822656 | tf_op jit(solution)/shard_map/dot_general | solution.py:19
  171.9 18.1 %all-to-all-done.1 = bf16[16,32,1280]{2,1,0:T(8,128)(2,1)} async-done(((bf16[16,32,1280]{2,1,0:T(8,128)(2,1)}), bf16[16,32,1280]{2,1,0:T(8,128)(2,1)}, u32[]{:S(2)}, u32[]{:S(2)}) %all-to-all-start.1) | async-done | bytes 1310752 | tf_op jit(solution)/shard_map/all_to_all | solution.py:102
  190.0 8.0 %all-to-all-start.3 = ((bf16[16,32,1280]{2,1,0:T(8,128)(2,1)}), bf16[16,32,1280]{2,1,0:T(8,128)(2,1)S(1)}, u32[]{:S(2)}, u32[]{:S(2)}) async-start(bf16[16,32,1280]{2,1,0:T(8,128)(2,1)} %bitcast.82), calls=%async_computation.3 | async-start | bytes 2621440 | tf_op jit(solution)/shard_map/all_to_all | solution.py:109
  198.1 4.7 %scatter_custom_fusion = bf16[512,1280]{1,0:T(8,128)(2,1)} fusion(s32[512]{0:T(512)S(1)} %bitcast.99, bf16[512,1280]{1,0:T(8,128)(2,1)} %bitcast.11, bf16[]{:T(256)} %constant.18.clone.1), kind=kCustom, calls=%fused_computation.50 | custom fusion | bytes 1311232 | tf_op jit(solution)/shard_map/scatter | solution.py:46
  202.8 39.8 %all-to-all-done.3 = bf16[16,32,1280]{2,1,0:T(8,128)(2,1)S(1)} async-done(((bf16[16,32,1280]{2,1,0:T(8,128)(2,1)}), bf16[16,32,1280]{2,1,0:T(8,128)(2,1)S(1)}, u32[]{:S(2)}, u32[]{:S(2)}) %all-to-all-start.3) | async-done | bytes 1310752 | tf_op jit(solution)/shard_map/all_to_all | solution.py:109
  242.6 4.2 %scatter_custom_fusion.1 = bf16[512,1280]{1,0:T(8,128)(2,1)} fusion(s32[512]{0:T(512)S(1)} %bitcast.100, bf16[512,1280]{1,0:T(8,128)(2,1)S(1)} %bitcast.98, bf16[]{:T(256)} %constant.18.clone.1), kind=kCustom, calls=%fused_computation.48 | custom fusion | bytes 1310722 | tf_op jit(solution)/shard_map/scatter | solution.py:46
  246.7 66.7 %reduce-scatter.3.cloned.1.call-done = f32[80,1920]{1,0:T(8,128)} async-done(((f32[1280,1920]{1,0:T(8,128)}), f32[80,1920]{1,0:T(8,128)}) %reduce-scatter.3.cloned.1.call-update) | async-done | bytes 614416 | tf_op jit(solution)/shard_map/reduce_scatter | solution.py:92
  (43 shorter events, 19.6 us)
Async XLA Ops:
  7.2 89.2 %copy-start = (bf16[640,1280]{1,0:T(8,128)(2,1)S(1)}, bf16[640,1280]{1,0:T(8,128)(2,1)}, u32[]{:S(2)}) copy-start(bf16[640,1280]{1,0:T(8,128)(2,1)} %param.14) | copy-start | bytes 4915204
  8.8 5.5 %copy-start.1 = (bf16[512,1280]{1,0:T(8,128)(2,1)S(1)}, bf16[512,1280]{1,0:T(8,128)(2,1)}, u32[]{:S(2)}) copy-start(bf16[512,1280]{1,0:T(8,128)(2,1)} %param.9) | copy-start | bytes 3932164
  21.0 7.5 %copy-start.7 = (s32[512]{0:T(512)S(1)}, s32[512]{0:T(512)}, u32[]{:S(2)}) copy-start(s32[512]{0:T(512)} %param.11) | copy-start | bytes 6148
  21.0 34.9 %all-to-all-start = ((bf16[16,32,1280]{2,1,0:T(8,128)(2,1)}), bf16[16,32,1280]{2,1,0:T(8,128)(2,1)S(1)}, u32[]{:S(2)}, u32[]{:S(2)}) async-start(bf16[16,32,1280]{2,1,0:T(8,128)(2,1)} %get-tuple-element.6), calls=%async_computation | async-start | bytes 2621440 | tf_op jit(solution)/shard_map/all_to_all | solution.py:49
  56.0 8.7 %copy-start.6 = (f32[1280]{0:T(1024)S(1)}, f32[1280]{0:T(1024)}, u32[]{:S(2)}) copy-start(f32[1280]{0:T(1024)} %param.12) | copy-start | bytes 15364
  56.0 35.7 %all-to-all-start.2 = ((bf16[16,32,1280]{2,1,0:T(8,128)(2,1)}), bf16[16,32,1280]{2,1,0:T(8,128)(2,1)}, u32[]{:S(2)}, u32[]{:S(2)}) async-start(bf16[16,32,1280]{2,1,0:T(8,128)(2,1)} %get-tuple-element.5), calls=%async_computation.2 | async-start | bytes 2621440 | tf_op jit(solution)/shard_map/all_to_all | solution.py:50
  64.1 182.6 %reduce-scatter.5.cloned.1.call-start = ((), (), s32[]{:S(2)}) async-start(), calls=%async_computation.7 | async-start | bytes 3481600 | tf_op jit(solution)/shard_map/reduce_scatter | solution.py:93
  96.1 217.3 %reduce-scatter.3.cloned.1.call-start = ((), (), s32[]{:S(2)}) async-start(), calls=%async_computation.6 | async-start | bytes 10444800 | tf_op jit(solution)/shard_map/reduce_scatter | solution.py:92
  139.1 5.2 %copy-start.3 = (bf16[512,1,8,80]{0,3,2,1:T(8,128)(2,1)S(1)}, bf16[512,1,8,80]{0,3,2,1:T(8,128)(2,1)}, u32[]{:S(2)}) copy-start(bf16[512,1,8,80]{0,3,2,1:T(8,128)(2,1)} %fusion.23) | copy-start | bytes 1966084
  139.1 5.2 %copy-start.4 = (bf16[512,1,8,80]{0,3,2,1:T(8,128)(2,1)S(1)}, bf16[512,1,8,80]{0,3,2,1:T(8,128)(2,1)}, u32[]{:S(2)}) copy-start(bf16[512,1,8,80]{0,3,2,1:T(8,128)(2,1)} %fusion.20) | copy-start | bytes 1966084
  144.5 1.3 copy-start.2
  154.6 35.4 %all-to-all-start.1 = ((bf16[16,32,1280]{2,1,0:T(8,128)(2,1)}), bf16[16,32,1280]{2,1,0:T(8,128)(2,1)}, u32[]{:S(2)}, u32[]{:S(2)}) async-start(bf16[16,32,1280]{2,1,0:T(8,128)(2,1)} %bitcast.97), calls=%async_computation.1 | async-start | bytes 2621440 | tf_op jit(solution)/shard_map/all_to_all | solution.py:102
  171.9 26.2 %copy-start.5 = (s32[1,16,32]{2,1,0:T(8,128)S(1)}, s32[1,16,32]{2,1,0:T(8,128)}, u32[]{:S(2)}) copy-start(s32[1,16,32]{2,1,0:T(8,128)} %param.10) | copy-start | bytes 6148
  190.0 52.6 %all-to-all-start.3 = ((bf16[16,32,1280]{2,1,0:T(8,128)(2,1)}), bf16[16,32,1280]{2,1,0:T(8,128)(2,1)S(1)}, u32[]{:S(2)}, u32[]{:S(2)}) async-start(bf16[16,32,1280]{2,1,0:T(8,128)(2,1)} %bitcast.82), calls=%async_computation.3 | async-start | bytes 2621440 | tf_op jit(solution)/shard_map/all_to_all | solution.py:109
Sparse Core Ops, SparseCore 0:
  96.2 70.1 reduce-scatter.4
  171.7 141.7 reduce-scatter.2
where the time goes:
time: 321 us; the launch traced here: 320 us
  waiting for transfers between devices  155 us (48%)
  matrix products  84.7 us (26%)
  starting transfers between devices  31.9 us (10%)
  local copies, waits for them, and re-layouts  24.6 us (8%)
  between operations  14.2 us (4%)
  other arithmetic  10 us (3%)
    reduce_scatter x1, waiting for transfers between devices, shards(): lax.psum_scatter(qkv_term, 'dp', scatter_dimension=0, tiled=True)  66.7 us
    all_to_all x1, waiting for transfers between devices, shards(): lax.all_to_all(d_rows.reshape(peer_count, per_peer, width), 'dp', split_a...  39.8 us
    all_to_all x1, waiting for transfers between devices, shards(): lax.all_to_all(pack(patches), 'dp', split_axis=0, concat_axis=0, tiled=True)  27.2 us
    all_to_all x1, waiting for transfers between devices, shards(): lax.all_to_all(mixed.reshape(peer_count, per_peer, width), 'dp', split_ax...  18.1 us
    dot_general x1, matrix products, shards(): jnp.einsum('hqk,qhd->khd', d_scores, queries, preferred_element_type=jnp....  15.9 us
    dot_general x1, matrix products, shards(): jnp.einsum('hqk,khd->qhd', d_scores, keys, preferred_element_type=jnp.flo...  15.5 us
    dot_general x2, matrix products, contract_rows(): lax.dot_general(left, right, (((0,), (0,)), ((), ())), preferred_element_...  9.84 us
    dot_general x2, matrix products, contract_cols(): lax.dot_general(left, right, (((1,), (1,)), ((), ())), preferred_element_...  9.58 us
  transfers between devices with their start and end apart: 6, of which 5 were waited for; matrix products, arithmetic and copies ran while one was open for 31% of the time, Pallas kernels for 0%

commit v1 on v0

--- a/solution.py
+++ b/solution.py
@@ -1,8 +1,11 @@
+import functools
 import math
 
 import jax
 import jax.numpy as jnp
 from jax import lax
+from jax.experimental import pallas as pl
+from jax.experimental.pallas import tpu as pltpu
 from jax.sharding import PartitionSpec as P
 
 HEADS = 8
@@ -119,6 +122,280 @@
     return (embeds, patch_grad, qkv_grad, proj_grad)
 
 
+MESH = pl.DeviceIdType.MESH
+F32, BF16 = jnp.float32, jnp.bfloat16
+
+
+def rev(value, bits):
+    out = 0
+    for _ in range(bits):
+        out = out * 2 + value % 2
+        value = value // 2
+    return out
+
+
+def mm(left, right):
+    return jnp.dot(left, right, preferred_element_type=F32)
+
+
+def block_kernel(
+    n, idx_col, idx_row, wid_col, wid_row, gain, patches, out_grad, w_qkv, w_proj,
+    embeds, patch_grad, qkv_out, proj_out,
+    packed, landed, back, normed, tall, qkvh, atth, flat, inv, term, inbox,
+    a_send, a_recv, r_send, r_recv,
+):
+    me = lax.axis_index("dp")
+    slots, width = patches.shape
+    cap = slots // n
+    bits = n.bit_length() - 1
+    inner = w_proj.shape[0]
+    own = width // n
+    scale = 1.0 / math.sqrt(HDIM)
+    grad_scale = 1.0 / math.sqrt(slots * n)
+
+    barrier = pltpu.get_barrier_semaphore()
+
+    def greet(k, carry):
+        pl.semaphore_signal(
+            barrier, inc=1, device_id={"dp": lax.rem(me + k, n)}, device_id_type=MESH
+        )
+        return carry
+
+    lax.fori_loop(1, n, greet, 0)
+
+    def rows_of(p):
+        return pl.ds(pl.multiple_of(p * cap, cap), cap)
+
+    def row_copy(src, dst, t, k):
+        peer = lax.rem(me + k, n)
+        return pltpu.make_async_remote_copy(
+            src_ref=src.at[rows_of(peer)],
+            dst_ref=dst.at[rows_of(me)],
+            send_sem=a_send.at[t, k],
+            recv_sem=a_recv.at[t, k],
+            device_id={"dp": peer},
+            device_id_type=MESH,
+        )
+
+    def send_rows(src, dst, t):
+        def go(k, carry):
+            row_copy(src, dst, t, k).start()
+            return carry
+
+        lax.fori_loop(1, n, go, 0)
+        dst[rows_of(me), :] = src[rows_of(me), :]
+
+    def recv_rows(src, dst, t):
+        def go(k, carry):
+            row_copy(src, dst, t, k).wait_recv()
+            return carry
+
+        lax.fori_loop(1, n, go, 0)
+
+    def sent_rows(src, dst, t):
+        def go(k, carry):
+            row_copy(src, dst, t, k).wait_send()
+            return carry
+
+        lax.fori_loop(1, n, go, 0)
+
+    def share_copy(c, step):
+        half = n >> (step + 1)
+        base = 0
+        for s in range(step):
+            base = base + lax.rem(me // (1 << s), 2) * (n >> (s + 1))
+        bit = lax.rem(me // (1 << step), 2)
+        peer = me + (1 << step) * (1 - 2 * bit)
+        away = base + (1 - bit) * half
+        kept = base + bit * half
+        copy = pltpu.make_async_remote_copy(
+            src_ref=term.at[c, pl.ds(away, half)],
+            dst_ref=inbox.at[c, pl.ds(half, half)],
+            send_sem=r_send.at[c, step],
+            recv_sem=r_recv.at[c, step],
+            device_id={"dp": peer},
+            device_id_type=MESH,
+        )
+        return copy, kept, half
+
+    def share_start(c, step):
+        share_copy(c, step)[0].start()
+
+    def share_add(c, step):
+        copy, kept, half = share_copy(c, step)
+        copy.wait_recv()
+
+        def add(i, carry):
+            term[c, kept + i] = term[c, kept + i] + inbox[c, half + i]
+            return carry
+
+        lax.fori_loop(0, half, add, 0)
+
+    def advance(c, step):
+        share_add(c, step)
+        if step + 1 < bits:
+            share_start(c, step + 1)
+
+    def make_term(c, left, right):
+        group = 4
+        for g in range(n // group):
+            part = mm(left[g * group * own:(g + 1) * group * own, :], right) * grad_scale
+            for i in range(group):
+                term[c, rev(g * group + i, bits)] = part[i * own:(i + 1) * own, :]
+
+    lanes = lax.broadcasted_iota(jnp.int32, (slots, slots), 1)
+    pick = jnp.where(lanes == idx_col[...], 1.0, 0.0).astype(BF16)
+    packed[0] = mm(pick, patches[...]).astype(BF16)
+    pl.semaphore_wait(barrier, n - 1)
+    send_rows(packed.at[0], landed.at[0], 0)
+    packed[1] = mm(pick, out_grad[...]).astype(BF16)
+    send_rows(packed.at[1], landed.at[1], 1)
+
+    recv_rows(packed.at[0], landed.at[0], 0)
+    row_vals = landed[0].astype(F32)
+    inv[...] = lax.rsqrt(jnp.mean(row_vals * row_vals, axis=-1, keepdims=True) + 1e-06)
+    normed[...] = (row_vals * inv[...] * gain[...]).astype(BF16)
+    for kind in range(3):
+        part = mm(normed[...], w_qkv[:, kind * inner:(kind + 1) * inner]).astype(BF16)
+        for h in range(HEADS):
+            qkvh[kind, h] = part[:, h * HDIM:(h + 1) * HDIM]
+
+    def probs_of(h):
+        scores = contract_cols(qkvh[0, h], qkvh[1, h]) * scale
+        scores = jnp.where(wid_col[...] == wid_row[...], scores, -1e30)
+        expo = jnp.exp(scores - jnp.max(scores, axis=-1, keepdims=True))
+        return expo * (1.0 / jnp.sum(expo, axis=-1, keepdims=True))
+
+    def forward(h, carry):
+        atth[h] = mm(probs_of(h).astype(BF16), qkvh[2, h]).astype(BF16)
+        return carry
+
+    lax.fori_loop(0, HEADS, forward, 0)
+    for h in range(HEADS):
+        flat[0, :, h * HDIM:(h + 1) * HDIM] = atth[h]
+    sent_rows(packed.at[0], landed.at[0], 0)
+    packed[0] = (landed[0].astype(F32) + mm(flat[0], w_proj[...])).astype(BF16)
+    send_rows(packed.at[0], back.at[0], 2)
+
+    recv_rows(packed.at[1], landed.at[1], 1)
+    tall[...] = landed[1].T
+    make_term(0, tall, flat[0])
+    share_start(0, 0)
+    tall[...] = normed[...].T
+    part = contract_cols(landed[1], w_proj[...]).astype(BF16)
+    for h in range(HEADS):
+        atth[h] = part[:, h * HDIM:(h + 1) * HDIM]
+
+    def backward(h, carry):
+        probs = probs_of(h)
+        grad = contract_cols(atth[h], qkvh[2, h])
+        dsc = probs * (grad - jnp.sum(probs * grad, axis=-1, keepdims=True)) * scale
+        dsc = dsc.astype(BF16)
+        d_query = mm(dsc, qkvh[1, h]).astype(BF16)
+        d_key = contract_rows(dsc, qkvh[0, h]).astype(BF16)
+        d_value = contract_rows(probs.astype(BF16), atth[h]).astype(BF16)
+        qkvh[0, h] = d_query
+        qkvh[1, h] = d_key
+        qkvh[2, h] = d_value
+        return carry
+
+    lax.fori_loop(0, HEADS // 2, backward, 0)
+    advance(0, 0)
+    lax.fori_loop(HEADS // 2, HEADS, backward, 0)
+    for kind in range(3):
+        for h in range(HEADS):
+            flat[kind, :, h * HDIM:(h + 1) * HDIM] = qkvh[kind, h]
+        make_term(kind + 1, tall, flat[kind])
+        share_start(kind + 1, 0)
+    advance(0, 1)
+    d_normed = contract_cols(flat[0], w_qkv[:, 0:inner])
+    for kind in range(1, 3):
+        d_normed = d_normed + contract_cols(
+            flat[kind], w_qkv[:, kind * inner:(kind + 1) * inner]
+        )
+    scaled = d_normed * gain[...]
+    unit = landed[0].astype(F32) * inv[...]
+    d_rows = landed[1].astype(F32) + inv[...] * (
+        scaled - unit * jnp.mean(scaled * unit, axis=-1, keepdims=True)
+    )
+    sent_rows(packed.at[1], landed.at[1], 1)
+    packed[1] = d_rows.astype(BF16)
+    send_rows(packed.at[1], back.at[1], 3)
+
+    for kind in range(3):
+        advance(kind + 1, 0)
+    advance(0, 2)
+    rows = lax.broadcasted_iota(jnp.int32, (slots, slots), 0)
+    place = jnp.where(rows == idx_row[...], 1.0, 0.0).astype(BF16)
+    recv_rows(packed.at[0], back.at[0], 2)
+    embeds[...] = mm(place, back[0]).astype(BF16)
+    for kind in range(3):
+        advance(kind + 1, 1)
+    advance(0, 3)
+    for step in range(2, bits):
+        for kind in range(3):
+            advance(kind + 1, step)
+    recv_rows(packed.at[1], back.at[1], 3)
+    patch_grad[...] = mm(place, back[1]).astype(BF16)
+    mine = 0
+    for s in range(bits):
+        mine = mine + lax.rem(me // (1 << s), 2) * (n >> (s + 1))
+    proj_out[...] = term[0, mine]
+    for kind in range(3):
+        qkv_out[:, kind * inner:(kind + 1) * inner] = term[kind + 1, mine]
+    sent_rows(packed.at[0], back.at[0], 2)
+    sent_rows(packed.at[1], back.at[1], 3)
+    for c in range(4):
+        for step in range(bits):
+            share_copy(c, step)[0].wait_send()
+
+
+def block(patches, send_index, window_id, norm_gain, w_qkv, w_proj, out_grad):
+    n = lax.axis_size("dp")
+    slots, width = patches.shape
+    inner = w_proj.shape[0]
+    own = width // n
+    bits = n.bit_length() - 1
+    vmem = pl.BlockSpec(memory_space=pltpu.VMEM)
+    rows = send_index.reshape(-1)
+    dma = pltpu.SemaphoreType.DMA
+    embeds, patch_grad, qkv_grad, proj_grad = pl.pallas_call(
+        functools.partial(block_kernel, n),
+        out_shape=(
+            jax.ShapeDtypeStruct((slots, width), BF16),
+            jax.ShapeDtypeStruct((slots, width), BF16),
+            jax.ShapeDtypeStruct((own, 3 * inner), F32),
+            jax.ShapeDtypeStruct((own, inner), F32),
+        ),
+        in_specs=[vmem] * 9,
+        out_specs=[vmem] * 4,
+        scratch_shapes=[
+            pltpu.VMEM((2, slots, width), BF16),
+            pltpu.VMEM((2, slots, width), BF16),
+            pltpu.VMEM((2, slots, width), BF16),
+            pltpu.VMEM((slots, width), BF16),
+            pltpu.VMEM((width, slots), BF16),
+            pltpu.VMEM((3, HEADS, slots, HDIM), BF16),
+            pltpu.VMEM((HEADS, slots, HDIM), BF16),
+            pltpu.VMEM((3, slots, inner), BF16),
+            pltpu.VMEM((slots, 1), F32),
+            pltpu.VMEM((4, n, own, inner), F32),
+            pltpu.VMEM((4, n, own, inner), F32),
+            dma((4, n)),
+            dma((4, n)),
+            dma((4, bits)),
+            dma((4, bits)),
+        ],
+        compiler_params=pltpu.CompilerParams(
+            collective_id=0, has_side_effects=True, vmem_limit_bytes=62 * 1024 * 1024
+        ),
+    )(
+        rows[:, None], rows[None, :], window_id[:, None], window_id[None, :],
+        norm_gain[None, :], patches, out_grad, w_qkv, w_proj,
+    )
+    return embeds, patch_grad, qkv_grad, proj_grad.T
+
+
 def solution(mesh):
     in_specs = (
         P(("groups", "dp"), None),
@@ -135,4 +412,15 @@
         P(("groups", "dp"), None),
         P("groups", "dp"),
     )
-    return jax.shard_map(shards, mesh=mesh, in_specs=in_specs, out_specs=out_specs, check_vma=False)
+
+    n = mesh.shape["dp"]
+
+    def run(patches, send_index, *rest):
+        width = patches.shape[1]
+        fits = send_index.shape[2] % 16 == 0 and n & (n - 1) == 0 and width % (8 * n) == 0
+        return jax.shard_map(
+            block if fits else shards,
+            mesh=mesh, in_specs=in_specs, out_specs=out_specs, check_vma=False,
+        )(patches, send_index, *rest)
+
+    return run

time: 321 us -> 228 us (0.71)
  the two profiles are of different devices: /device:TPU:0 before, /device:TPU:5 now
where the time goes in v1:
time: 228 us
  Pallas kernels  216 us (95%)
  local copies, waits for them, and re-layouts  11.4 us (5%)
    pallas_call x1, Pallas kernels, block(): pl.pallas_call(functools.partial(block_kernel, n), out_shape=(jax.ShapeDt...  216 us
    unnamed x10, local copies, waits for them, and re-layouts  5.54 us

profile of v1, /device:TPU:5, one launch (start us, length us, event | category | flops | bytes accessed | tf_op | source)
XLA Modules:
  0.0 227.6 jit_solution(1108117340103527657)
XLA Ops:
  0.6 1.4 broadcast_in_dim_reshape.7.idx_row
  2.0 1.3 broadcast_in_dim.11.gain
  3.3 1.5 copy.12.wid_col
  4.8 1.7 broadcast_in_dim_reshape.8.idx_col
  6.5 215.6 %shard_map.102 = (bf16[512,1280]{1,0:T(8,128)(2,1)}, bf16[512,1280]{1,0:T(8,128)(2,1)}, f32[80,1920]{1,0:T(8,128)}, f32[80,640]{1,0:T(8,128)}) custom-call(s32[512,1]{1,0:T(8,128)} %broadcast_in_dim_reshape.8.idx_col, s32[1,512]{1,0:T(1,128)} %broadcast_in_dim_reshape.7.idx_row, s32[512,1]{1,0:T(8,128)} %copy.12.wid_col, s32[1,512]{1,0:T(1,128)} %bitcast.5, ...), custom_call_target="tpu_custom_call" | custom-call | tf_op jit(solution)/shard_map/pallas_call | solution.py:362
  222.0 0.0 copy-start
  222.1 2.6 %copy.17 = bf16[512,1280]{1,0:T(8,128)(2,1)} copy(bf16[512,1280]{1,0:T(8,128)(2,1)} %get-tuple-element.16) | data formatting | bytes 2621440
  224.6 0.0 copy-done
  224.6 0.0 copy-start.1
  224.6 0.0 copy-start.2
  224.6 1.1 copy.18
  225.7 0.4 copy-done.1
  226.1 0.8 copy.19
  226.9 0.0 copy-done.2
  226.9 0.7 copy.20
Async XLA Ops:
  222.0 2.6 %copy-start = (bf16[512,1280]{1,0:T(8,128)(2,1)S(1)}, bf16[512,1280]{1,0:T(8,128)(2,1)}, u32[]{:S(2)}) copy-start(bf16[512,1280]{1,0:T(8,128)(2,1)} %get-tuple-element.17) | copy-start | bytes 3932164
  224.6 1.5 copy-start.1
  224.6 2.3 %copy-start.2 = (f32[80,640]{1,0:T(8,128)S(1)}, f32[80,640]{1,0:T(8,128)}, u32[]{:S(2)}) copy-start(f32[80,640]{1,0:T(8,128)} %get-tuple-element.11) | copy-start | bytes 614404

commit v2 on v1

--- a/solution.py
+++ b/solution.py
@@ -139,10 +139,10 @@
 
 
 def block_kernel(
-    n, idx_col, idx_row, wid_col, wid_row, gain, patches, out_grad, w_qkv, w_proj,
+    n, send_index, window_id, norm_gain, patches, out_grad, w_qkv, w_proj,
     embeds, patch_grad, qkv_out, proj_out,
-    packed, landed, back, normed, tall, qkvh, atth, flat, inv, term, inbox,
-    a_send, a_recv, r_send, r_recv,
+    packed, landed, back, att, batt, normed, tall, qkvh, atth, flat, inv, gain, idx_row, wid_row,
+    wid_col, term, inbox, outbox, in_scale, out_scale, a_send, a_recv, r_send, r_recv,
 ):
     me = lax.axis_index("dp")
     slots, width = patches.shape
@@ -199,34 +199,53 @@
 
         lax.fori_loop(1, n, go, 0)
 
-    def share_copy(c, step):
+    def share_place(step):
         half = n >> (step + 1)
         base = 0
         for s in range(step):
             base = base + lax.rem(me // (1 << s), 2) * (n >> (s + 1))
         bit = lax.rem(me // (1 << step), 2)
         peer = me + (1 << step) * (1 - 2 * bit)
-        away = base + (1 - bit) * half
-        kept = base + bit * half
-        copy = pltpu.make_async_remote_copy(
-            src_ref=term.at[c, pl.ds(away, half)],
-            dst_ref=inbox.at[c, pl.ds(half, half)],
-            send_sem=r_send.at[c, step],
-            recv_sem=r_recv.at[c, step],
-            device_id={"dp": peer},
-            device_id_type=MESH,
-        )
-        return copy, kept, half
+        return peer, base + (1 - bit) * half, base + bit * half, half
+
+    def share_copies(c, step):
+        peer, _, _, half = share_place(step)
+        part = pl.ds(half, half)
+        return [
+            pltpu.make_async_remote_copy(
+                src_ref=source.at[c, part],
+                dst_ref=target.at[c, part],
+                send_sem=r_send.at[c, step, kind],
+                recv_sem=r_recv.at[c, step, kind],
+                device_id={"dp": peer},
+                device_id_type=MESH,
+            )
+            for kind, (source, target) in enumerate(((outbox, inbox), (out_scale, in_scale)))
+        ]
 
     def share_start(c, step):
-        share_copy(c, step)[0].start()
+        _, away, _, half = share_place(step)
+
+        def code(i, carry):
+            value = term[c, away + i]
+            most = jnp.max(jnp.abs(value), axis=0, keepdims=True)
+            factor = jnp.where(most > 1e-30, 32767.0 / jnp.maximum(most, 1e-30), 0.0)
+            outbox[c, half + i] = jnp.round(value * factor).astype(jnp.int32).astype(jnp.int16)
+            out_scale[c, half + i] = most * (1.0 / 32767.0)
+            return carry
+
+        lax.fori_loop(0, half, code, 0)
+        for copy in share_copies(c, step):
+            copy.start()
 
     def share_add(c, step):
-        copy, kept, half = share_copy(c, step)
-        copy.wait_recv()
+        _, _, kept, half = share_place(step)
+        for copy in share_copies(c, step):
+            copy.wait_recv()
 
         def add(i, carry):
-            term[c, kept + i] = term[c, kept + i] + inbox[c, half + i]
+            value = inbox[c, half + i].astype(jnp.int32).astype(F32)
+            term[c, kept + i] = term[c, kept + i] + value * in_scale[c, half + i]
             return carry
 
         lax.fori_loop(0, half, add, 0)
@@ -243,12 +262,17 @@
             for i in range(group):
                 term[c, rev(g * group + i, bits)] = part[i * own:(i + 1) * own, :]
 
-    lanes = lax.broadcasted_iota(jnp.int32, (slots, slots), 1)
-    pick = jnp.where(lanes == idx_col[...], 1.0, 0.0).astype(BF16)
-    packed[0] = mm(pick, patches[...]).astype(BF16)
+    for p in range(n):
+        idx_row[0:1, p * cap:(p + 1) * cap] = send_index[0, p:p + 1, :]
+    wid_row[...] = window_id[...].reshape(1, slots)
+    gain[...] = norm_gain[...].reshape(1, width)
+    wid_col[...] = jnp.broadcast_to(wid_row[...], (128, slots)).T[:, 0:1]
+    rows = lax.broadcasted_iota(jnp.int32, (slots, slots), 0)
+    place = jnp.where(rows == idx_row[...], 1.0, 0.0).astype(BF16)
+    packed[0] = contract_rows(place, patches[...]).astype(BF16)
     pl.semaphore_wait(barrier, n - 1)
     send_rows(packed.at[0], landed.at[0], 0)
-    packed[1] = mm(pick, out_grad[...]).astype(BF16)
+    packed[1] = contract_rows(place, out_grad[...]).astype(BF16)
     send_rows(packed.at[1], landed.at[1], 1)
 
     recv_rows(packed.at[0], landed.at[0], 0)
@@ -272,14 +296,12 @@
 
     lax.fori_loop(0, HEADS, forward, 0)
     for h in range(HEADS):
-        flat[0, :, h * HDIM:(h + 1) * HDIM] = atth[h]
-    sent_rows(packed.at[0], landed.at[0], 0)
-    packed[0] = (landed[0].astype(F32) + mm(flat[0], w_proj[...])).astype(BF16)
-    send_rows(packed.at[0], back.at[0], 2)
+        att[:, h * HDIM:(h + 1) * HDIM] = atth[h]
+    send_rows(att, batt, 2)
 
     recv_rows(packed.at[1], landed.at[1], 1)
     tall[...] = landed[1].T
-    make_term(0, tall, flat[0])
+    make_term(0, tall, att[...])
     share_start(0, 0)
     tall[...] = normed[...].T
     part = contract_cols(landed[1], w_proj[...]).astype(BF16)
@@ -320,34 +342,38 @@
     )
     sent_rows(packed.at[1], landed.at[1], 1)
     packed[1] = d_rows.astype(BF16)
-    send_rows(packed.at[1], back.at[1], 3)
+    send_rows(packed.at[1], back, 3)
 
     for kind in range(3):
         advance(kind + 1, 0)
     advance(0, 2)
-    rows = lax.broadcasted_iota(jnp.int32, (slots, slots), 0)
-    place = jnp.where(rows == idx_row[...], 1.0, 0.0).astype(BF16)
-    recv_rows(packed.at[0], back.at[0], 2)
-    embeds[...] = mm(place, back[0]).astype(BF16)
+    place = jnp.where(rows == idx_row[...], 1.0, 0.0)
+    live = jnp.sum(place, axis=-1, keepdims=True)
+    place = place.astype(BF16)
+    recv_rows(att, batt, 2)
+    home = mm(place, batt[...]).astype(BF16)
+    embeds[...] = (patches[...].astype(F32) * live + mm(home, w_proj[...])).astype(BF16)
     for kind in range(3):
         advance(kind + 1, 1)
     advance(0, 3)
     for step in range(2, bits):
         for kind in range(3):
             advance(kind + 1, step)
-    recv_rows(packed.at[1], back.at[1], 3)
-    patch_grad[...] = mm(place, back[1]).astype(BF16)
+    recv_rows(packed.at[1], back, 3)
+    patch_grad[...] = mm(place, back[...]).astype(BF16)
     mine = 0
     for s in range(bits):
         mine = mine + lax.rem(me // (1 << s), 2) * (n >> (s + 1))
     proj_out[...] = term[0, mine]
     for kind in range(3):
         qkv_out[:, kind * inner:(kind + 1) * inner] = term[kind + 1, mine]
-    sent_rows(packed.at[0], back.at[0], 2)
-    sent_rows(packed.at[1], back.at[1], 3)
+    sent_rows(packed.at[0], landed.at[0], 0)
+    sent_rows(att, batt, 2)
+    sent_rows(packed.at[1], back, 3)
     for c in range(4):
         for step in range(bits):
-            share_copy(c, step)[0].wait_send()
+            for copy in share_copies(c, step):
+                copy.wait_send()
 
 
 def block(patches, send_index, window_id, norm_gain, w_qkv, w_proj, out_grad):
@@ -357,7 +383,6 @@
     own = width // n
     bits = n.bit_length() - 1
     vmem = pl.BlockSpec(memory_space=pltpu.VMEM)
-    rows = send_index.reshape(-1)
     dma = pltpu.SemaphoreType.DMA
     embeds, patch_grad, qkv_grad, proj_grad = pl.pallas_call(
         functools.partial(block_kernel, n),
@@ -367,31 +392,39 @@
             jax.ShapeDtypeStruct((own, 3 * inner), F32),
             jax.ShapeDtypeStruct((own, inner), F32),
         ),
-        in_specs=[vmem] * 9,
+        in_specs=[vmem] * 7,
         out_specs=[vmem] * 4,
         scratch_shapes=[
             pltpu.VMEM((2, slots, width), BF16),
             pltpu.VMEM((2, slots, width), BF16),
-            pltpu.VMEM((2, slots, width), BF16),
+            pltpu.VMEM((slots, width), BF16),
+            pltpu.VMEM((slots, inner), BF16),
+            pltpu.VMEM((slots, inner), BF16),
             pltpu.VMEM((slots, width), BF16),
             pltpu.VMEM((width, slots), BF16),
             pltpu.VMEM((3, HEADS, slots, HDIM), BF16),
             pltpu.VMEM((HEADS, slots, HDIM), BF16),
             pltpu.VMEM((3, slots, inner), BF16),
             pltpu.VMEM((slots, 1), F32),
+            pltpu.VMEM((1, width), F32),
+            pltpu.VMEM((1, slots), jnp.int32),
+            pltpu.VMEM((1, slots), jnp.int32),
+            pltpu.VMEM((slots, 1), jnp.int32),
             pltpu.VMEM((4, n, own, inner), F32),
-            pltpu.VMEM((4, n, own, inner), F32),
+            pltpu.VMEM((4, n, own, inner), jnp.int16),
+            pltpu.VMEM((4, n, own, inner), jnp.int16),
+            pltpu.VMEM((4, n, 1, inner), F32),
+            pltpu.VMEM((4, n, 1, inner), F32),
             dma((4, n)),
             dma((4, n)),
-            dma((4, bits)),
-            dma((4, bits)),
+            dma((4, bits, 2)),
+            dma((4, bits, 2)),
         ],
         compiler_params=pltpu.CompilerParams(
             collective_id=0, has_side_effects=True, vmem_limit_bytes=62 * 1024 * 1024
         ),
     )(
-        rows[:, None], rows[None, :], window_id[:, None], window_id[None, :],
-        norm_gain[None, :], patches, out_grad, w_qkv, w_proj,
+        send_index, window_id, norm_gain, patches, out_grad, w_qkv, w_proj,
     )
     return embeds, patch_grad, qkv_grad, proj_grad.T
 

time: 228 us -> 169 us (0.74)
  the two profiles are of different devices: /device:TPU:5 before, /device:TPU:0 now
where the time goes in v2:
time: 169 us; the launch traced here: 168 us
  Pallas kernels  162 us (96%)
  local copies, waits for them, and re-layouts  5.54 us (3%)
    pallas_call x1, Pallas kernels, block(): pl.pallas_call(functools.partial(block_kernel, n), out_shape=(jax.ShapeDt...  162 us
    unnamed x10, local copies, waits for them, and re-layouts  5.54 us

profile of v2, /device:TPU:0, one launch (start us, length us, event | category | flops | bytes accessed | tf_op | source)
XLA Modules:
  0.0 168.3 jit_solution(14000591432350209844)
XLA Ops:
  0.6 162.1 %shard_map.102 = (bf16[512,1280]{1,0:T(8,128)(2,1)}, bf16[512,1280]{1,0:T(8,128)(2,1)}, f32[80,1920]{1,0:T(8,128)}, f32[80,640]{1,0:T(8,128)}) custom-call(s32[1,16,32]{2,1,0:T(8,128)} %send_index.1, s32[512]{0:T(512)} %window_id.1, f32[1280]{0:T(1024)} %norm_gain.1, bf16[512,1280]{1,0:T(8,128)(2,1)} %patches.1, bf16[512,1280]{1,0:T(8,128)(2,1)} %out_grad.1, ...), custom_call_target="tpu_custom_call" | custom-call | tf_op jit(solution)/shard_map/pallas_call | solution.py:387
  162.8 0.0 copy-start
  162.8 2.6 %copy.15 = bf16[512,1280]{1,0:T(8,128)(2,1)} copy(bf16[512,1280]{1,0:T(8,128)(2,1)} %get-tuple-element.16) | data formatting | bytes 2621440
  165.4 0.0 copy-done
  165.4 0.0 copy-start.1
  165.4 0.0 copy-start.2
  165.4 1.1 copy.16
  166.4 0.4 copy-done.1
  166.8 0.8 copy.17
  167.7 0.0 copy-done.2
  167.7 0.7 copy.18
Async XLA Ops:
  162.8 2.6 %copy-start = (bf16[512,1280]{1,0:T(8,128)(2,1)S(1)}, bf16[512,1280]{1,0:T(8,128)(2,1)}, u32[]{:S(2)}) copy-start(bf16[512,1280]{1,0:T(8,128)(2,1)} %get-tuple-element.17) | copy-start | bytes 3932164
  165.4 1.5 copy-start.1
  165.4 2.3 %copy-start.2 = (f32[80,640]{1,0:T(8,128)S(1)}, f32[80,640]{1,0:T(8,128)}, u32[]{:S(2)}) copy-start(f32[80,640]{1,0:T(8,128)} %get-tuple-element.11) | copy-start | bytes 614404
